TPU v7x, 32 devices: a whole 2x2x4 slice. The times are simulated.
32 devices in a mesh: inter: 8 (over y, x, core), intra: 4 (over z).
Axes of the slice: x: 2, y: 2, z: 4, core: 2. Of those that a mesh axis runs over, the one named last changes fastest.
Arguments:
- layer_input: bfloat16 [6144, 3584], P(('inter', 'intra')), may hold values from -6 to 6
- up_cotangent: bfloat16 [6144, 10240], P(('inter', 'intra')), may hold values from -6 to 6
- master: float32 [10240, 3584], P(('intra', 'inter')), may hold values from -0.6 to 0.6
- first_moment: float32 [10240, 3584], P(('intra', 'inter')), may hold values from -6 to 6
- second_moment: float32 [10240, 3584], P(('intra', 'inter')), may hold values from 0.2 to 0.5
Outputs:
- new_master: float32 [10240, 3584], P(('intra', 'inter'))
- new_first: float32 [10240, 3584], P(('intra', 'inter'))
- new_second: float32 [10240, 3584], P(('intra', 'inter'))
- new_copy: bfloat16 [10240, 3584], P('intra')
All inputs are finite; a program needn't handle non-finite values.
Results may differ from a plain program's by a relative error of at most 0.015.
Values may be sent and summed in bfloat16 or wider, within the bound.
A program may use at most 192 MiB of HBM per device.

v0:
```python
import math

import jax
import jax.numpy as jnp
from jax import lax
from jax.sharding import PartitionSpec as P


def adamw(grad, master, first_moment, second_moment):
    new_first = 0.9 * first_moment + 0.1 * grad
    new_second = 0.95 * second_moment + 0.05 * (grad * grad)
    first_hat = new_first / (1.0 - 0.9**10)
    second_hat = new_second / (1.0 - 0.95**10)
    step_dir = first_hat / (jnp.sqrt(second_hat) + 1e-08) + 0.1 * master
    new_master = master - 0.02 * step_dir
    return (new_master, new_first, new_second)


def body(layer_input, up_cotangent, master, first_moment, second_moment):
    local_tokens = layer_input.shape[0]
    inter_count = lax.axis_size("inter")
    intra_count = lax.axis_size("intra")
    total_tokens = local_tokens * inter_count * intra_count
    contract = (((0,), (0,)), ((), ()))
    hidden_part = lax.all_to_all(up_cotangent, "intra", split_axis=1, concat_axis=0, tiled=True)
    gathered = lax.all_gather(layer_input, "intra", axis=0, tiled=True)
    summed = lax.psum_scatter(
        lax.dot_general(hidden_part, gathered, contract, preferred_element_type=jnp.float32).astype(
            jnp.bfloat16
        ),
        "inter",
        scatter_dimension=0,
        tiled=True,
    ).astype(jnp.float32)
    grad = summed * (1.0 / math.sqrt(total_tokens))
    new_master, new_first, new_second = adamw(grad, master, first_moment, second_moment)
    new_copy = lax.all_gather(new_master.astype(jnp.bfloat16), "inter", axis=0, tiled=True)
    return (new_master, new_first, new_second, new_copy)


def solution(mesh):
    in_specs = (
        P(("inter", "intra"), None),
        P(("inter", "intra"), None),
        P(("intra", "inter"), None),
        P(("intra", "inter"), None),
        P(("intra", "inter"), None),
    )
    out_specs = (
        P(("intra", "inter"), None),
        P(("intra", "inter"), None),
        P(("intra", "inter"), None),
        P("intra", None),
    )
    return jax.shard_map(body, mesh=mesh, in_specs=in_specs, out_specs=out_specs, check_vma=False)
```

profile of v0, /device:TPU:9, one launch (start us, length us, event | category | flops | bytes accessed | tf_op | source)
XLA Modules:
  0.0 466.0 jit_solution(7909428192748346165)
XLA Ops:
  7.2 0.0 all-gather.3.cloned.1.call-start
  7.2 0.7 all-gather.3.cloned.1.call-update
  7.9 0.0 reduce-scatter.2.cloned.1.call-start
  7.9 2.5 copy.13
  10.4 172.6 %all_to_all.19 = bf16[192,4,2560]{2,0,1:T(8,128)(2,1)} all-to-all(bf16[192,4,2560]{2,0,1:T(8,128)(2,1)S(1)} %bitcast.9), channel_id=1, replica_groups=mesh['inter'=8,'intra'=4] {'intra'}, dimensions={1} | all-to-all | bytes 7864320 | tf_op jit(solution)/shard_map/all_to_all | solution.py:25
  183.1 5.5 %all-gather.3.cloned.1.call-done = bf16[768,3584]{1,0:T(8,128)(2,1)} async-done(((bf16[192,3584]{1,0:T(8,128)(2,1)}), bf16[768,3584]{1,0:T(8,128)(2,1)}) %all-gather.3.cloned.1.call-update) | async-done | bytes 5505040 | tf_op jit(solution)/shard_map/all_gather | solution.py:26
  188.5 21.4 %convolution_convert_fusion = bf16[2560,3584]{1,0:T(8,128)(2,1)} fusion(bf16[768,2560]{1,0:T(8,128)(2,1)} %bitcast.11, bf16[768,3584]{1,0:T(8,128)(2,1)} %all-gather.3.cloned.1.call-done), kind=kOutput, calls=%fused_computation | convolution fusion | flops 14102036480 | bytes 27787264 | tf_op jit(solution)/shard_map/dot_general | solution.py:28
  209.9 0.0 reduce-scatter.2.cloned.1.call-update
  209.9 0.0 all-gather.5.cloned.1.call-start
  210.0 125.3 %reduce-scatter.2.cloned.1.call-done = bf16[320,3584]{1,0:T(8,128)(2,1)} async-done(((bf16[2560,3584]{1,0:T(8,128)(2,1)}), bf16[320,3584]{1,0:T(8,128)(2,1)}) %reduce-scatter.2.cloned.1.call-update) | async-done | bytes 2293776 | tf_op jit(solution)/shard_map/reduce_scatter | solution.py:27
  335.3 11.1 %fusion.4 = (bf16[320,3584]{1,0:T(8,128)(2,1)}, f32[320,3584]{1,0:T(8,128)}, f32[320,3584]{1,0:T(8,128)}, f32[320,3584]{1,0:T(8,128)}) fusion(f32[320,3584]{1,0:T(8,128)} %param.7, bf16[320,3584]{1,0:T(8,128)(2,1)} %reduce-scatter.2.cloned.1.call-done, f32[320,3584]{1,0:T(8,128)} %param.8, f32[320,3584]{1,0:T(8,128)} %param.9), kind=kLoop, calls=%fused_computation.9 | loop fusion | flops 20643840 | bytes 32112640 | tf_op jit(solution)/shard_map/convert_element_type | solution.py:37
  346.3 0.0 all-gather.5.cloned.1.call-update
  346.3 97.1 %all-gather.5.cloned.1.call-done = bf16[2560,3584]{1,0:T(8,128)(2,1)} async-done(((bf16[320,3584]{1,0:T(8,128)(2,1)}), bf16[2560,3584]{1,0:T(8,128)(2,1)}) %all-gather.5.cloned.1.call-update) | async-done | bytes 18350096 | tf_op jit(solution)/shard_map/all_gather | solution.py:37
  443.5 16.0 %copy.15 = bf16[2560,3584]{1,0:T(8,128)(2,1)} copy(bf16[2560,3584]{1,0:T(8,128)(2,1)} %all-gather.5.cloned.1.call-done) | data formatting | bytes 36700160
Async XLA Ops:
  7.2 181.4 %all-gather.3.cloned.1.call-start = ((), (), s32[]{:S(2)}) async-start(), calls=%async_computation.2 | async-start | bytes 6881280 | tf_op jit(solution)/shard_map/all_gather | solution.py:26
  7.9 327.4 %reduce-scatter.2.cloned.1.call-start = ((), (), s32[]{:S(2)}) async-start(), calls=%async_computation.3 | async-start | bytes 20643840 | tf_op jit(solution)/shard_map/reduce_scatter | solution.py:27
  209.9 233.5 %all-gather.5.cloned.1.call-start = ((), (), s32[]{:S(2)}) async-start(), calls=%async_computation.4 | async-start | bytes 20643840 | tf_op jit(solution)/shard_map/all_gather | solution.py:37
Sparse Core Ops, SparseCore 0:
  9.6 178.9 all-gather.2
  210.0 125.1 reduce-scatter.1
  346.5 96.9 all-gather.4
where the time goes:
time: 467 us; the launch traced here: 466 us
  waiting for transfers between devices  229 us (49%)
  blocking collectives  173 us (37%)
  matrix products  21.4 us (5%)
  local copies, waits for them, and re-layouts  18.5 us (4%)
  between operations  13.8 us (3%)
  other arithmetic  11.1 us (2%)
    all_to_all x1, blocking collectives, body(): lax.all_to_all(up_cotangent, 'intra', split_axis=1, concat_axis=0, tiled=...  173 us
    reduce_scatter x1, waiting for transfers between devices, body(): lax.psum_scatter(lax.dot_general(hidden_part, gathered, contract, preferr...  125 us
    all_gather x1, waiting for transfers between devices, body(): lax.all_gather(new_master.astype(jnp.bfloat16), 'inter', axis=0, tiled=True)  97.1 us
    dot_general x1, matrix products, body(): lax.dot_general(hidden_part, gathered, contract, preferred_element_type=j...  21.4 us
    unnamed x1, local copies, waits for them, and re-layouts  16 us
    convert_element_type x1, other arithmetic, body(): new_master.astype(jnp.bfloat16)  11.1 us
  transfers between devices with their start and end apart: 3, of which 3 were waited for; matrix products, arithmetic and copies ran while one was open for 1% of the time, Pallas kernels for 0%

commit v1 on v0

v1 whole, which is shorter than its diff:
```python
import functools
import math

import jax
import jax.numpy as jnp
from jax import lax
from jax.experimental import pallas as pl
from jax.experimental.pallas import tpu as pltpu
from jax.sharding import PartitionSpec as P

MESH = pl.DeviceIdType.MESH
STEP = 16


def kernel(
    n, m, group, parts,
    x_ref, cot_ref, m_in, f_in, s_in,
    m_out, f_out, s_out, c_out,
    xg, cg, tr, outb, mine, sib, rs, mbuf, fbuf, sbuf, cbuf,
    x_local, x_send, x_recv, c_local, c_send, c_recv, sib_send, sib_recv,
    rs_send, rs_recv, in_sem, out_sem, ag_send, ag_recv, own_sem, fw_send, fw_recv,
):
    i = lax.axis_index("inter")
    j = lax.axis_index("intra")
    tok, cols = x_ref.shape
    rows = m_in.shape[0]
    nc = m // 2
    core = lax.rem(i, 2)
    chip = i // 2
    other = 1 - core
    sibling = {"inter": chip * 2 + other}
    width = group * 2 * rows
    per_intra = m * rows
    pieces = rows // parts
    scale = 1.0 / math.sqrt(tok * n * m)

    def same_core(c):
        return {"inter": c * 2 + core}

    barrier = pltpu.get_barrier_semaphore()
    for d in range(1, n):
        pl.semaphore_signal(barrier, inc=1, device_id={"intra": lax.rem(j + d, n)}, device_id_type=MESH)
    pl.semaphore_signal(barrier, inc=1, device_id=sibling, device_id_type=MESH)
    for d in range(1, nc):
        pl.semaphore_signal(barrier, inc=1, device_id=same_core(lax.rem(chip + d, nc)), device_id_type=MESH)
    pl.semaphore_wait(barrier, n - 1 + 1 + nc - 1)

    def x_slot(s):
        return xg.at[pl.ds(pl.multiple_of(s * tok, tok), tok), :]

    def x_copy(way, t):
        s = j - t if way == 0 else j + t
        to = j + 1 if way == 0 else j - 1
        return pltpu.make_async_remote_copy(
            src_ref=x_ref if t == 0 else x_slot(s), dst_ref=x_slot(s),
            send_sem=x_send.at[way, t], recv_sem=x_recv.at[way, t],
            device_id={"intra": to}, device_id_type=MESH)

    def x_sends(way, t):
        if way == 0:
            return jnp.logical_and(j - t >= 0, j + 1 < n)
        return jnp.logical_and(j + t < n, j >= 1)

    def x_gets(way, t):
        if way == 0:
            return j - 1 - t >= 0
        return j + 1 + t < n

    def x_arrival(way, t):
        s = j - 1 - t if way == 0 else j + 1 + t
        return pltpu.make_async_remote_copy(
            src_ref=x_slot(s), dst_ref=x_slot(s),
            send_sem=x_send.at[way, t], recv_sem=x_recv.at[way, t],
            device_id={"intra": lax.rem(j + 1, n)}, device_id_type=MESH)

    def part_of(t):
        return lax.rem(chip // group + 1 + t, nc // group)

    def cot_copy(t, d):
        to = lax.rem(j + d, n)
        start = pl.multiple_of(to * per_intra + part_of(t) * width, 128)
        return pltpu.make_async_remote_copy(
            src_ref=cot_ref.at[:, pl.ds(start, width)],
            dst_ref=cg.at[t, pl.ds(pl.multiple_of(j * tok, tok), tok), :],
            send_sem=c_send.at[t, d - 1], recv_sem=c_recv.at[t, d - 1],
            device_id={"intra": to}, device_id_type=MESH)

    def cot_local(t):
        start = pl.multiple_of(j * per_intra + part_of(t) * width, 128)
        return pltpu.make_async_copy(
            cot_ref.at[:, pl.ds(start, width)],
            cg.at[t, pl.ds(pl.multiple_of(j * tok, tok), tok), :],
            c_local.at[t])

    for way in range(2):
        @pl.when(x_sends(way, 0))
        def _():
            x_copy(way, 0).start()
    own_x = pltpu.make_async_copy(x_ref, x_slot(j), x_local)
    own_x.start()
    state = [(m_in, mbuf), (f_in, fbuf), (s_in, sbuf)]
    for t in range(nc // group):
        cot_local(t).start()
    for t in range(1, n):
        for way in range(2):
            @pl.when(x_gets(way, t - 1))
            def _():
                x_arrival(way, t - 1).wait_recv()
            if t < n - 1:
                @pl.when(x_sends(way, t))
                def _():
                    x_copy(way, t).start()
        if t == max(n - 2, 1):
            for s in range(nc // group):
                for d in range(1, n):
                    cot_copy(s, d).start()
    for k, (src, dst) in enumerate(state):
        pltpu.make_async_copy(src, dst, in_sem.at[k]).start()
    own_x.wait()

    tile = 512 if cols % 512 == 0 else 128

    def product(dst, off):
        @pl.loop(0, cols // tile)
        def _(k):
            c0 = pl.multiple_of(k * tile, tile)
            dst[:, pl.ds(c0, tile)] = jnp.dot(
                tr[pl.ds(pl.multiple_of(off, 16), rows), :], xg[:, pl.ds(c0, tile)],
                preferred_element_type=jnp.float32).astype(jnp.bfloat16)

    def sib_copy(e):
        return pltpu.make_async_remote_copy(
            src_ref=outb.at[e % 2], dst_ref=sib.at[e],
            send_sem=sib_send.at[e], recv_sem=sib_recv.at[e],
            device_id=sibling, device_id_type=MESH)

    def rs_copy(e, q, d):
        return pltpu.make_async_remote_copy(
            src_ref=mine.at[e], dst_ref=rs.at[d - 1],
            send_sem=rs_send.at[d - 1], recv_sem=rs_recv.at[d - 1],
            device_id=same_core(q), device_id_type=MESH)

    for t in range(nc // group):
        cot_local(t).wait()
        for d in range(1, n):
            cot_copy(t, d).wait_recv()
        tr[...] = cg[t].T
        for u in range(group):
            e = t * group + u
            if e >= 2:
                sib_copy(e - 2).wait_send()
            product(outb.at[e % 2], (2 * u + other) * rows)
            sib_copy(e).start()
            product(mine.at[e], (2 * u + core) * rows)
            sib_copy(e).wait_recv()
            q = part_of(t) * group + u
            d = lax.rem(q - chip + nc, nc)

            @pl.loop(0, rows // STEP)
            def _(k):
                at = pl.ds(pl.multiple_of(k * STEP, STEP), STEP)
                mine[e, at, :] = (mine[e, at, :].astype(jnp.float32) + sib[e, at, :].astype(jnp.float32)).astype(jnp.bfloat16)

            @pl.when(d != 0)
            def _():
                rs_copy(e, q, d).start()

    for k, (src, dst) in enumerate(state):
        pltpu.make_async_copy(src, dst, in_sem.at[k]).wait()
    last = (nc // group - 1) * group + lax.rem(chip, group)
    for d in range(1, nc):
        rs_copy(0, lax.rem(chip + d, nc), d).wait_recv()

    def out_rows(owner, r):
        return c_out.at[pl.ds(pl.multiple_of(owner * rows + r * pieces, 16), pieces), :]

    def ag_copy(r, d):
        to = sibling if d == 0 else same_core(lax.rem(chip + d, nc))
        return pltpu.make_async_remote_copy(
            src_ref=cbuf.at[pl.ds(r * pieces, pieces), :], dst_ref=out_rows(i, r),
            send_sem=ag_send.at[r, d], recv_sem=ag_recv.at[r, d],
            device_id=to, device_id_type=MESH)

    def forward(r, d):
        from_chip = lax.rem(chip - d + nc, nc)
        ref = out_rows(from_chip * 2 + core, r)
        return pltpu.make_async_remote_copy(
            src_ref=ref, dst_ref=ref,
            send_sem=fw_send.at[r, d - 1], recv_sem=fw_recv.at[r, d - 1],
            device_id=sibling, device_id_type=MESH)

    def own_copy(r):
        return pltpu.make_async_copy(cbuf.at[pl.ds(r * pieces, pieces), :], out_rows(i, r), own_sem.at[r])

    def state_out(r, k):
        src = (mbuf, fbuf, sbuf)[k].at[pl.ds(r * pieces, pieces), :]
        dst = (m_out, f_out, s_out)[k].at[pl.ds(r * pieces, pieces), :]
        return pltpu.make_async_copy(src, dst, out_sem.at[r, k])

    for r in range(parts):
        @pl.loop(0, pieces // STEP)
        def _(k):
            at = pl.ds(pl.multiple_of(r * pieces + k * STEP, STEP), STEP)
            total = mine[last, at, :].astype(jnp.float32)
            for d in range(nc - 1):
                total = total + rs[d, at, :].astype(jnp.float32)
            grad = total * scale
            master = mbuf[at, :]
            new_first = 0.9 * fbuf[at, :] + 0.1 * grad
            new_second = 0.95 * sbuf[at, :] + 0.05 * (grad * grad)
            first_hat = new_first / (1.0 - 0.9**10)
            second_hat = new_second / (1.0 - 0.95**10)
            step_dir = first_hat / (jnp.sqrt(second_hat) + 1e-08) + 0.1 * master
            new_master = master - 0.02 * step_dir
            mbuf[at, :] = new_master
            fbuf[at, :] = new_first
            sbuf[at, :] = new_second
            cbuf[at, :] = new_master.astype(jnp.bfloat16)

        for d in (*range(1, nc), 0):
            ag_copy(r, d).start()
        own_copy(r).start()
        for k in range(3):
            state_out(r, k).start()

    for r in range(parts):
        for d in range(1, nc):
            ag_copy(r, d).wait_recv()
            forward(r, d).start()
    for r in range(parts):
        ag_copy(r, 0).wait_recv()
        own_copy(r).wait()
        for k in range(3):
            state_out(r, k).wait()
        for d in range(1, nc):
            forward(r, d).wait_recv()
            forward(r, d).wait_send()
        for d in range(nc):
            ag_copy(r, d).wait_send()
    for way in range(2):
        for t in range(n - 1):
            @pl.when(x_sends(way, t))
            def _():
                x_copy(way, t).wait_send()
    for t in range(nc // group):
        for d in range(1, n):
            cot_copy(t, d).wait_send()
    for e in range(max(nc - 2, 0), nc):
        sib_copy(e).wait_send()
    for d in range(1, nc):
        rs_copy(0, lax.rem(chip + d, nc), d).wait_send()


def body(n, m, layer_input, up_cotangent, master, first_moment, second_moment):
    tok, cols = layer_input.shape
    rows = master.shape[0]
    nc = m // 2
    group = 1
    while (group * 2 * rows) % 128:
        group *= 2
    count = nc // group
    parts = 5
    bf, f32 = jnp.bfloat16, jnp.float32
    dma = pltpu.SemaphoreType.DMA
    state = jax.ShapeDtypeStruct((rows, cols), f32)
    return pl.pallas_call(
        functools.partial(kernel, n, m, group, parts),
        out_shape=(state, state, state, jax.ShapeDtypeStruct((m * rows, cols), bf)),
        in_specs=[pl.BlockSpec(memory_space=pl.ANY)] * 5,
        out_specs=[pl.BlockSpec(memory_space=pl.ANY)] * 4,
        scratch_shapes=[
            pltpu.VMEM((n * tok, cols), bf),
            pltpu.VMEM((count, n * tok, group * 2 * rows), bf),
            pltpu.VMEM((group * 2 * rows, n * tok), bf),
            pltpu.VMEM((2, rows, cols), bf),
            pltpu.VMEM((nc, rows, cols), bf),
            pltpu.VMEM((nc, rows, cols), bf),
            pltpu.VMEM((nc - 1, rows, cols), bf),
            pltpu.VMEM((rows, cols), f32),
            pltpu.VMEM((rows, cols), f32),
            pltpu.VMEM((rows, cols), f32),
            pltpu.VMEM((rows, cols), bf),
            dma, dma((2, n)), dma((2, n)),
            dma((count,)), dma((count, n - 1)), dma((count, n - 1)),
            dma((nc,)), dma((nc,)),
            dma((nc - 1,)), dma((nc - 1,)),
            dma((3,)), dma((parts, 3)),
            dma((parts, nc)), dma((parts, nc)),
            dma((parts,)),
            dma((parts, nc - 1)), dma((parts, nc - 1)),
        ],
        compiler_params=pltpu.CompilerParams(
            collective_id=0, has_side_effects=True, vmem_limit_bytes=60 * 1024 * 1024),
        cost_estimate=pl.CostEstimate(
            flops=2 * n * tok * m * rows * cols, bytes_accessed=60_000_000, transcendentals=rows * cols),
    )(layer_input, up_cotangent, master, first_moment, second_moment)


def solution(mesh):
    split = P(("inter", "intra"), None)
    owned = P(("intra", "inter"), None)
    return jax.shard_map(
        functools.partial(body, mesh.shape["intra"], mesh.shape["inter"]), mesh=mesh,
        in_specs=(split, split, owned, owned, owned),
        out_specs=(owned, owned, owned, P("intra", None)), check_vma=False)
```

time: 467 us -> 386 us (0.83)
  Pallas kernels: 0 us -> 363 us
  waiting for transfers between devices: 229 us -> 0 us
  blocking collectives: 173 us -> 0 us
  matrix products: 21.4 us -> 0 us
  between operations: 13.8 us -> 0.66 us
  other arithmetic: 11.1 us -> 0 us
    pallas_call x0 -> x1, Pallas kernels: none -> 363 us  [body(): pl.pallas_call(functools.partial(kernel, n, m, group, parts), out_shape=(...]
    all_to_all x1 -> x0, blocking collectives: 173 us -> none  [body(): lax.all_to_all(up_cotangent, 'intra', split_axis=1, concat_axis=0, tiled=...]
    reduce_scatter x1 -> x0, waiting for transfers between devices: 125 us -> none  [body(): lax.psum_scatter(lax.dot_general(hidden_part, gathered, contract, preferr...]
    all_gather x2 -> x0, waiting for transfers between devices: 103 us -> none  [the longest x1 97.1 us: body(): lax.all_gather(new_master.astype(jnp.bfloat16), 'inter', axis=0, tiled=True)]
    dot_general x1 -> x0, matrix products: 21.4 us -> none  [body(): lax.dot_general(hidden_part, gathered, contract, preferred_element_type=j...]
    convert_element_type x1 -> x0, other arithmetic: 11.1 us -> none  [body(): new_master.astype(jnp.bfloat16)]
    unnamed x1 -> x10, local copies, waits for them, and re-layouts: 16 us -> 22.1 us
  transfers between devices with their start and end apart: 3 -> 0, of which waited for: 3 -> 0; matrix products, arithmetic and copies ran while one was open for 1% -> 0% of each run, Pallas kernels for 0% -> 0%
where the time goes in v1:
time: 386 us; the launch traced here: 385 us
  Pallas kernels  363 us (94%)
  local copies, waits for them, and re-layouts  22.1 us (6%)
    pallas_call x1, Pallas kernels, body(): pl.pallas_call(functools.partial(kernel, n, m, group, parts), out_shape=(...  363 us
    unnamed x10, local copies, waits for them, and re-layouts  22.1 us

profile of v1, /device:TPU:9, one launch (start us, length us, event | category | flops | bytes accessed | tf_op | source)
XLA Modules:
  0.0 385.4 jit_solution(3105384951213436917)
XLA Ops:
  0.6 362.7 %shard_map.84 = (f32[320,3584]{1,0:T(8,128)}, f32[320,3584]{1,0:T(8,128)}, f32[320,3584]{1,0:T(8,128)}, bf16[2560,3584]{1,0:T(8,128)(2,1)}) custom-call(bf16[192,3584]{1,0:T(8,128)(2,1)} %x_ref.1, bf16[192,10240]{1,0:T(8,128)(2,1)} %cot_ref.1, f32[320,3584]{1,0:T(8,128)} %m_in.1, f32[320,3584]{1,0:T(8,128)} %f_in.1, f32[320,3584]{1,0:T(8,128)} %s_in.1), custom_call_target="tpu_custom_call" | custom-call | flops 14092861440 | bytes 60000000 | tf_op jit(solution)/shard_map/pallas_call | solution.py:266
  363.3 0.0 copy-start.2
  363.3 0.0 copy-start.1
  363.3 5.1 %copy.13 = f32[320,3584]{1,0:T(8,128)} copy(f32[320,3584]{1,0:T(8,128)} %get-tuple-element.8) | data formatting | bytes 9175040
  368.4 0.0 copy-done.2
  368.4 0.0 copy-start
  368.4 2.3 copy.14
  370.8 0.8 copy-done.1
  371.5 2.3 copy.15
  373.8 4.9 %copy-done = bf16[2560,3584]{1,0:T(8,128)(2,1)S(1)} copy-done((bf16[2560,3584]{1,0:T(8,128)(2,1)S(1)}, bf16[2560,3584]{1,0:T(8,128)(2,1)}, u32[]{:S(2)}) %copy-start) | copy-done | bytes 18350104
  378.7 6.7 %copy.16 = bf16[2560,3584]{1,0:T(8,128)(2,1)} copy(bf16[2560,3584]{1,0:T(8,128)(2,1)S(1)} %copy-done) | data formatting | bytes 36700160
Async XLA Ops:
  363.3 5.1 %copy-start.2 = (f32[320,3584]{1,0:T(8,128)S(1)}, f32[320,3584]{1,0:T(8,128)}, u32[]{:S(2)}) copy-start(f32[320,3584]{1,0:T(8,128)} %get-tuple-element.9) | copy-start | bytes 13762564
  363.3 8.2 %copy-start.1 = (f32[320,3584]{1,0:T(8,128)S(1)}, f32[320,3584]{1,0:T(8,128)}, u32[]{:S(2)}) copy-start(f32[320,3584]{1,0:T(8,128)} %get-tuple-element.10) | copy-start | bytes 13762564
  368.4 10.3 %copy-start = (bf16[2560,3584]{1,0:T(8,128)(2,1)S(1)}, bf16[2560,3584]{1,0:T(8,128)(2,1)}, u32[]{:S(2)}) copy-start(bf16[2560,3584]{1,0:T(8,128)(2,1)} %get-tuple-element.11) | copy-start | bytes 55050244

commit v2 on v1

v2 whole, which is shorter than its diff:
```python
import functools
import math

import jax
import jax.numpy as jnp
from jax import lax
from jax.experimental import pallas as pl
from jax.experimental.pallas import tpu as pltpu
from jax.sharding import PartitionSpec as P

MESH = pl.DeviceIdType.MESH
STEP = 16


def kernel(
    n, m, group, parts, blocks,
    x_ref, cot_ref, m_in, f_in, s_in,
    m_out, f_out, s_out, c_out,
    xg, cg, tr, outb, mine, sib, rs, mbuf, fbuf, sbuf, cbuf,
    x_local, x_send, x_recv, c_local, c_send, c_recv, sib_send, sib_recv,
    rs_send, rs_recv, in_sem, out_sem, ag_send, ag_recv, own_sem, fw_send, fw_recv,
):
    i = lax.axis_index("inter")
    j = lax.axis_index("intra")
    tok, cols = x_ref.shape
    rows = m_in.shape[0]
    nc = m // 2
    core = lax.rem(i, 2)
    chip = i // 2
    other = 1 - core
    sibling = {"inter": chip * 2 + other}
    width = group * 2 * rows
    per_intra = m * rows
    pieces = rows // parts
    scale = 1.0 / math.sqrt(tok * n * m)

    def same_core(c):
        return {"inter": c * 2 + core}

    barrier = pltpu.get_barrier_semaphore()
    for d in range(1, n):
        pl.semaphore_signal(barrier, inc=1, device_id={"intra": lax.rem(j + d, n)}, device_id_type=MESH)
    pl.semaphore_signal(barrier, inc=1, device_id=sibling, device_id_type=MESH)
    for d in range(1, nc):
        pl.semaphore_signal(barrier, inc=1, device_id=same_core(lax.rem(chip + d, nc)), device_id_type=MESH)
    pl.semaphore_wait(barrier, n - 1 + 1 + nc - 1)

    def at_cols(h):
        return pl.ds(*blocks[h])

    def x_slot(s, h):
        return xg.at[pl.ds(pl.multiple_of(s * tok, tok), tok), at_cols(h)]

    def x_copy(h, way, t):
        s = j - t if way == 0 else j + t
        to = j + 1 if way == 0 else j - 1
        return pltpu.make_async_remote_copy(
            src_ref=x_ref.at[:, at_cols(h)] if t == 0 else x_slot(s, h), dst_ref=x_slot(s, h),
            send_sem=x_send.at[h, way, t], recv_sem=x_recv.at[h, way, t],
            device_id={"intra": to}, device_id_type=MESH)

    def x_sends(way, t):
        if way == 0:
            return jnp.logical_and(j - t >= 0, j + 1 < n)
        return jnp.logical_and(j + t < n, j >= 1)

    def x_gets(way, t):
        if way == 0:
            return j - 1 - t >= 0
        return j + 1 + t < n

    def x_arrival(h, way, t):
        s = j - 1 - t if way == 0 else j + 1 + t
        return pltpu.make_async_remote_copy(
            src_ref=x_slot(s, h), dst_ref=x_slot(s, h),
            send_sem=x_send.at[h, way, t], recv_sem=x_recv.at[h, way, t],
            device_id={"intra": lax.rem(j + 1, n)}, device_id_type=MESH)

    def part_of(t):
        return lax.rem(chip // group + 1 + t, nc // group)

    def cot_copy(t, d):
        to = lax.rem(j + d, n)
        start = pl.multiple_of(to * per_intra + part_of(t) * width, 128)
        return pltpu.make_async_remote_copy(
            src_ref=cot_ref.at[:, pl.ds(start, width)],
            dst_ref=cg.at[t, pl.ds(pl.multiple_of(j * tok, tok), tok), :],
            send_sem=c_send.at[t, d - 1], recv_sem=c_recv.at[t, d - 1],
            device_id={"intra": to}, device_id_type=MESH)

    def cot_local(t):
        start = pl.multiple_of(j * per_intra + part_of(t) * width, 128)
        return pltpu.make_async_copy(
            cot_ref.at[:, pl.ds(start, width)],
            cg.at[t, pl.ds(pl.multiple_of(j * tok, tok), tok), :],
            c_local.at[t])

    def x_begin(h):
        for way in range(2):
            @pl.when(x_sends(way, 0))
            def _():
                x_copy(h, way, 0).start()

    def x_relay(h, t):
        for way in range(2):
            @pl.when(x_gets(way, t - 1))
            def _():
                x_arrival(h, way, t - 1).wait_recv()
            if t < n - 1:
                @pl.when(x_sends(way, t))
                def _():
                    x_copy(h, way, t).start()

    x_begin(0)
    own_x = pltpu.make_async_copy(x_ref, xg.at[pl.ds(pl.multiple_of(j * tok, tok), tok), :], x_local)
    own_x.start()
    state = [(m_in, mbuf), (f_in, fbuf), (s_in, sbuf)]
    for t in range(nc // group):
        cot_local(t).start()
    for t in range(1, n):
        x_relay(0, t)
        if t == max(n - 2, 1):
            for s in range(nc // group):
                for d in range(1, n):
                    cot_copy(s, d).start()
    for k, (src, dst) in enumerate(state):
        pltpu.make_async_copy(src, dst, in_sem.at[k]).start()
    own_x.wait()

    def product(dst, h, off):
        start, size = blocks[h]
        tile = 512 if size % 512 == 0 else 128

        @pl.loop(0, size // tile)
        def _(k):
            c0 = pl.multiple_of(start + k * tile, 128)
            dst[:, pl.ds(c0, tile)] = jnp.dot(
                tr[pl.ds(pl.multiple_of(off, 16), rows), :], xg[:, pl.ds(c0, tile)],
                preferred_element_type=jnp.float32).astype(jnp.bfloat16)

    def sib_copy(h, e):
        return pltpu.make_async_remote_copy(
            src_ref=outb.at[e % 2, :, at_cols(h)], dst_ref=sib.at[e, :, at_cols(h)],
            send_sem=sib_send.at[h, e], recv_sem=sib_recv.at[h, e],
            device_id=sibling, device_id_type=MESH)

    def rs_copy(h, e, q, d):
        return pltpu.make_async_remote_copy(
            src_ref=mine.at[e, :, at_cols(h)], dst_ref=rs.at[d - 1, :, at_cols(h)],
            send_sem=rs_send.at[h, d - 1], recv_sem=rs_recv.at[h, d - 1],
            device_id=same_core(q), device_id_type=MESH)

    def part_sums(h, t):
        tr[...] = cg[t].T
        for u in range(group):
            e = t * group + u
            if e >= 2:
                sib_copy(h, e - 2).wait_send()
            product(outb.at[e % 2], h, (2 * u + other) * rows)
            sib_copy(h, e).start()
            product(mine.at[e], h, (2 * u + core) * rows)
            sib_copy(h, e).wait_recv()
            q = part_of(t) * group + u
            d = lax.rem(q - chip + nc, nc)

            @pl.loop(0, rows // STEP)
            def _(k):
                at = pl.ds(pl.multiple_of(k * STEP, STEP), STEP)
                mine[e, at, at_cols(h)] = (
                    mine[e, at, at_cols(h)].astype(jnp.float32) + sib[e, at, at_cols(h)].astype(jnp.float32)
                ).astype(jnp.bfloat16)

            @pl.when(d != 0)
            def _():
                rs_copy(h, e, q, d).start()

    last = (nc // group - 1) * group + lax.rem(chip, group)

    def out_rows(h, owner, r):
        return c_out.at[pl.ds(pl.multiple_of(owner * rows + r * pieces, 16), pieces), at_cols(h)]

    def ag_copy(h, r, d):
        to = sibling if d == 0 else same_core(lax.rem(chip + d, nc))
        return pltpu.make_async_remote_copy(
            src_ref=cbuf.at[pl.ds(r * pieces, pieces), at_cols(h)], dst_ref=out_rows(h, i, r),
            send_sem=ag_send.at[h, r, d], recv_sem=ag_recv.at[h, r, d],
            device_id=to, device_id_type=MESH)

    def forward(h, r, d):
        from_chip = lax.rem(chip - d + nc, nc)
        ref = out_rows(h, from_chip * 2 + core, r)
        return pltpu.make_async_remote_copy(
            src_ref=ref, dst_ref=ref,
            send_sem=fw_send.at[h, r, d - 1], recv_sem=fw_recv.at[h, r, d - 1],
            device_id=sibling, device_id_type=MESH)

    def own_copy(h, r):
        return pltpu.make_async_copy(
            cbuf.at[pl.ds(r * pieces, pieces), at_cols(h)], out_rows(h, i, r), own_sem.at[h, r])

    def state_out(h, r, k):
        src = (mbuf, fbuf, sbuf)[k].at[pl.ds(r * pieces, pieces), at_cols(h)]
        dst = (m_out, f_out, s_out)[k].at[pl.ds(r * pieces, pieces), at_cols(h)]
        return pltpu.make_async_copy(src, dst, out_sem.at[h, r, k])

    def update(h):
        for d in range(1, nc):
            rs_copy(h, 0, lax.rem(chip + d, nc), d).wait_recv()
        cs = at_cols(h)
        for r in range(parts):
            @pl.loop(0, pieces // STEP)
            def _(k):
                at = pl.ds(pl.multiple_of(r * pieces + k * STEP, STEP), STEP)
                total = mine[last, at, cs].astype(jnp.float32)
                for d in range(nc - 1):
                    total = total + rs[d, at, cs].astype(jnp.float32)
                grad = total * scale
                master = mbuf[at, cs]
                new_first = 0.9 * fbuf[at, cs] + 0.1 * grad
                new_second = 0.95 * sbuf[at, cs] + 0.05 * (grad * grad)
                first_hat = new_first / (1.0 - 0.9**10)
                second_hat = new_second / (1.0 - 0.95**10)
                step_dir = first_hat / (jnp.sqrt(second_hat) + 1e-08) + 0.1 * master
                new_master = master - 0.02 * step_dir
                mbuf[at, cs] = new_master
                fbuf[at, cs] = new_first
                sbuf[at, cs] = new_second
                cbuf[at, cs] = new_master.astype(jnp.bfloat16)

            for d in (*range(1, nc), 0):
                ag_copy(h, r, d).start()
            own_copy(h, r).start()
            for k in range(3):
                state_out(h, r, k).start()

    def forwards(h):
        for r in range(parts):
            for d in range(1, nc):
                ag_copy(h, r, d).wait_recv()
                forward(h, r, d).start()

    def sums_sent(h):
        for e in range(max(nc - 2, 0), nc):
            sib_copy(h, e).wait_send()

    count = nc // group
    for t in range(count):
        cot_local(t).wait()
        for d in range(1, n):
            cot_copy(t, d).wait_recv()
        if t == max(count - 2, 0):
            x_begin(1)
        part_sums(0, t)
    sums_sent(0)
    x_relay(1, 1)
    for k, (src, dst) in enumerate(state):
        pltpu.make_async_copy(src, dst, in_sem.at[k]).wait()
    update(0)
    for t in range(2, n):
        x_relay(1, t)
    for t in range(count):
        part_sums(1, t)
    sums_sent(1)
    forwards(0)
    update(1)
    forwards(1)

    for h in range(len(blocks)):
        for r in range(parts):
            ag_copy(h, r, 0).wait_recv()
            own_copy(h, r).wait()
            for k in range(3):
                state_out(h, r, k).wait()
            for d in range(1, nc):
                forward(h, r, d).wait_recv()
                forward(h, r, d).wait_send()
            for d in range(nc):
                ag_copy(h, r, d).wait_send()
        for way in range(2):
            for t in range(n - 1):
                @pl.when(x_sends(way, t))
                def _():
                    x_copy(h, way, t).wait_send()
        for d in range(1, nc):
            rs_copy(h, 0, lax.rem(chip + d, nc), d).wait_send()
    for t in range(count):
        for d in range(1, n):
            cot_copy(t, d).wait_send()


def body(n, m, layer_input, up_cotangent, master, first_moment, second_moment):
    tok, cols = layer_input.shape
    rows = master.shape[0]
    nc = m // 2
    group = 1
    while (group * 2 * rows) % 128:
        group *= 2
    count = nc // group
    parts = 5
    first = cols // 128 * 4 // 7 * 128
    blocks = ((0, first), (first, cols - first))
    nb = len(blocks)
    bf, f32 = jnp.bfloat16, jnp.float32
    dma = pltpu.SemaphoreType.DMA
    state = jax.ShapeDtypeStruct((rows, cols), f32)
    return pl.pallas_call(
        functools.partial(kernel, n, m, group, parts, blocks),
        out_shape=(state, state, state, jax.ShapeDtypeStruct((m * rows, cols), bf)),
        in_specs=[pl.BlockSpec(memory_space=pl.ANY)] * 5,
        out_specs=[pl.BlockSpec(memory_space=pl.ANY)] * 4,
        scratch_shapes=[
            pltpu.VMEM((n * tok, cols), bf),
            pltpu.VMEM((count, n * tok, group * 2 * rows), bf),
            pltpu.VMEM((group * 2 * rows, n * tok), bf),
            pltpu.VMEM((2, rows, cols), bf),
            pltpu.VMEM((nc, rows, cols), bf),
            pltpu.VMEM((nc, rows, cols), bf),
            pltpu.VMEM((nc - 1, rows, cols), bf),
            pltpu.VMEM((rows, cols), f32),
            pltpu.VMEM((rows, cols), f32),
            pltpu.VMEM((rows, cols), f32),
            pltpu.VMEM((rows, cols), bf),
            dma, dma((nb, 2, n)), dma((nb, 2, n)),
            dma((count,)), dma((count, n - 1)), dma((count, n - 1)),
            dma((nb, nc)), dma((nb, nc)),
            dma((nb, nc - 1)), dma((nb, nc - 1)),
            dma((3,)), dma((nb, parts, 3)),
            dma((nb, parts, nc)), dma((nb, parts, nc)),
            dma((nb, parts)),
            dma((nb, parts, nc - 1)), dma((nb, parts, nc - 1)),
        ],
        compiler_params=pltpu.CompilerParams(
            collective_id=0, has_side_effects=True, vmem_limit_bytes=60 * 1024 * 1024),
        cost_estimate=pl.CostEstimate(
            flops=2 * n * tok * m * rows * cols, bytes_accessed=60_000_000, transcendentals=rows * cols),
    )(layer_input, up_cotangent, master, first_moment, second_moment)


def solution(mesh):
    split = P(("inter", "intra"), None)
    owned = P(("intra", "inter"), None)
    return jax.shard_map(
        functools.partial(body, mesh.shape["intra"], mesh.shape["inter"]), mesh=mesh,
        in_specs=(split, split, owned, owned, owned),
        out_specs=(owned, owned, owned, P("intra", None)), check_vma=False)
```

time: 386 us -> 352 us (0.912)
  Pallas kernels: 363 us -> 327 us
    pallas_call x1, Pallas kernels: 363 us -> 327 us  [body(): pl.pallas_call(functools.partial(kernel, n, m, group, parts, blocks), out...]
where the time goes in v2:
time: 352 us; the launch traced here: 349 us
  Pallas kernels  327 us (93%)
  local copies, waits for them, and re-layouts  22.1 us (6%)
    pallas_call x1, Pallas kernels, body(): pl.pallas_call(functools.partial(kernel, n, m, group, parts, blocks), out...  327 us
    unnamed x10, local copies, waits for them, and re-layouts  22.1 us

profile of v2, /device:TPU:9, one launch (start us, length us, event | category | flops | bytes accessed | tf_op | source)
XLA Modules:
  0.0 349.5 jit_solution(5015852239693554687)
XLA Ops:
  0.6 326.7 %shard_map.84 = (f32[320,3584]{1,0:T(8,128)}, f32[320,3584]{1,0:T(8,128)}, f32[320,3584]{1,0:T(8,128)}, bf16[2560,3584]{1,0:T(8,128)(2,1)}) custom-call(bf16[192,3584]{1,0:T(8,128)(2,1)} %x_ref.1, bf16[192,10240]{1,0:T(8,128)(2,1)} %cot_ref.1, f32[320,3584]{1,0:T(8,128)} %m_in.1, f32[320,3584]{1,0:T(8,128)} %f_in.1, f32[320,3584]{1,0:T(8,128)} %s_in.1), custom_call_target="tpu_custom_call" | custom-call | flops 14092861440 | bytes 60000000 | tf_op jit(solution)/shard_map/pallas_call | solution.py:306
  327.4 0.0 copy-start.2
  327.4 0.0 copy-start.1
  327.4 5.1 %copy.13 = f32[320,3584]{1,0:T(8,128)} copy(f32[320,3584]{1,0:T(8,128)} %get-tuple-element.8) | data formatting | bytes 9175040
  332.5 0.0 copy-done.2
  332.5 0.0 copy-start
  332.5 2.3 copy.14
  334.8 0.8 copy-done.1
  335.6 2.3 copy.15
  337.9 4.9 %copy-done = bf16[2560,3584]{1,0:T(8,128)(2,1)S(1)} copy-done((bf16[2560,3584]{1,0:T(8,128)(2,1)S(1)}, bf16[2560,3584]{1,0:T(8,128)(2,1)}, u32[]{:S(2)}) %copy-start) | copy-done | bytes 18350104
  342.8 6.7 %copy.16 = bf16[2560,3584]{1,0:T(8,128)(2,1)} copy(bf16[2560,3584]{1,0:T(8,128)(2,1)S(1)} %copy-done) | data formatting | bytes 36700160
Async XLA Ops:
  327.4 5.1 %copy-start.2 = (f32[320,3584]{1,0:T(8,128)S(1)}, f32[320,3584]{1,0:T(8,128)}, u32[]{:S(2)}) copy-start(f32[320,3584]{1,0:T(8,128)} %get-tuple-element.9) | copy-start | bytes 13762564
  327.4 8.2 %copy-start.1 = (f32[320,3584]{1,0:T(8,128)S(1)}, f32[320,3584]{1,0:T(8,128)}, u32[]{:S(2)}) copy-start(f32[320,3584]{1,0:T(8,128)} %get-tuple-element.10) | copy-start | bytes 13762564
  332.5 10.3 %copy-start = (bf16[2560,3584]{1,0:T(8,128)(2,1)S(1)}, bf16[2560,3584]{1,0:T(8,128)(2,1)}, u32[]{:S(2)}) copy-start(bf16[2560,3584]{1,0:T(8,128)(2,1)} %get-tuple-element.11) | copy-start | bytes 55050244
